TPU v7x, 256 devices: a whole 4x4x8 slice. The times are simulated.
256 devices in a mesh: blk: 32 (over z, y_hi, core), group: 8 (over x, y_lo).
Axes of the slice: x: 4, y: 4 (y_hi: 2, y_lo: 2; y = y_hi * 2 + y_lo), z: 8, core: 2. Of those that a mesh axis runs over, the one named last changes fastest.
Arguments:
- image_embed: bfloat16 [163840, 1152], P(('blk', 'group')), may hold values from -0.1796875 to 0.1796875
- text_embed: bfloat16 [163840, 1152], P(('blk', 'group')), may hold values from -0.1796875 to 0.1796875
- text_bits: int32 [163840, 1152], P(('blk', 'group')), may hold values from 0 to 4095
- labels: int32 [163840], replicated, may hold values from 0 to 2559
- scale: float32 [], replicated, may hold values from 4 to 12
- bias: float32 [], replicated, may hold values from -3 to -1
Outputs:
- grad_image: bfloat16 [163840, 1152], P(('blk', 'group'))
- grad_text: bfloat16 [163840, 1152], P(('blk', 'group'))
All inputs are finite; a program needn't handle non-finite values.
Results may differ from a plain program's by a relative error of at most 0.0065.
Values may be sent and summed in bfloat16 or wider, within the bound.
A program may use at most 128 MiB of HBM per device.

v0:
```python
import jax
import jax.numpy as jnp
from jax import lax
from jax.sharding import PartitionSpec as P

EPS = 1e-06


def with_halo(cells, sides, width):
    for axis, dim in sides:
        count = lax.axis_size(axis)
        head = lax.slice_in_dim(cells, 0, width, axis=dim)
        tail = lax.slice_in_dim(cells, cells.shape[dim] - width, cells.shape[dim], axis=dim)
        cells = jnp.concatenate(
            [
                lax.ppermute(tail, axis, [(i, (i + 1) % count) for i in range(count)]),
                cells,
                lax.ppermute(head, axis, [((i + 1) % count, i) for i in range(count)]),
            ],
            axis=dim,
        )
    return cells


def shifted(value, axis, steps):
    count = lax.axis_size(axis)
    pairs = [(source, (source + steps) % count) for source in range(count)]
    return lax.ppermute(value, axis, pairs)


def unit_rows(values):
    full = values.astype(jnp.float32)
    inverse = lax.rsqrt(jnp.sum(full * full, axis=-1, keepdims=True) + EPS)
    return (full * inverse, inverse)


def quantize(text_embed, text_bits):
    noise = (text_bits.astype(jnp.float32) + 0.5) / 4096.0
    return jnp.floor(text_embed.astype(jnp.float32) * 128.0 + noise) / 128.0


def pair_dot(left, right):
    return lax.dot_general(
        left, right, (((1,), (1,)), ((), ())), preferred_element_type=jnp.float32
    )


def column_dot(left, right):
    return lax.dot_general(
        left, right, (((0,), (0,)), ((), ())), preferred_element_type=jnp.float32
    )


def coefficient(left_half, right_half, left_labels, right_labels, scale, bias):
    logit = scale * pair_dot(left_half, right_half) + bias
    sign = jnp.where(left_labels[:, None] == right_labels[None, :], 1.0, -1.0).astype(jnp.float32)
    return (-sign * scale * jax.nn.sigmoid(-sign * logit)).astype(jnp.bfloat16)


def shards(image_embed, text_embed, text_bits, labels, scale, bias):
    num_rows = image_embed.shape[0]
    cycle_size = lax.axis_size("blk")
    group_size = lax.axis_size("group")
    cycle_pos = lax.axis_index("blk")
    group_pos = lax.axis_index("group")

    def labels_of(cycle_at, group_at):
        number = (cycle_at + cycle_size) % cycle_size * group_size + (
            group_at + group_size
        ) % group_size
        return lax.dynamic_slice_in_dim(labels, number * num_rows, num_rows)

    image_unit, image_inv = unit_rows(image_embed)
    text_unit, text_inv = unit_rows(quantize(text_embed, text_bits))
    image_half = image_unit.astype(jnp.bfloat16)
    text_half = text_unit.astype(jnp.bfloat16)
    own_labels = labels_of(cycle_pos, group_pos)
    below_labels = labels_of(cycle_pos - 1, group_pos)
    above_labels = labels_of(cycle_pos + 1, group_pos)
    cycle_text = with_halo(text_half, (("blk", 0),), num_rows)
    below_text = cycle_text[:num_rows]
    above_text = cycle_text[2 * num_rows :]
    handed_text = shifted(text_half, "group", 1)
    handed_labels = labels_of(cycle_pos, group_pos - 1)
    own_coef = coefficient(image_half, text_half, own_labels, own_labels, scale, bias)
    image_sum = jnp.dot(own_coef, text_half, preferred_element_type=jnp.float32)
    text_sum = column_dot(own_coef, image_half)
    below_coef = coefficient(image_half, below_text, own_labels, below_labels, scale, bias)
    above_coef = coefficient(image_half, above_text, own_labels, above_labels, scale, bias)
    handed_coef = coefficient(image_half, handed_text, own_labels, handed_labels, scale, bias)
    image_sum = image_sum + jnp.dot(below_coef, below_text, preferred_element_type=jnp.float32)
    image_sum = image_sum + jnp.dot(above_coef, above_text, preferred_element_type=jnp.float32)
    image_sum = image_sum + jnp.dot(handed_coef, handed_text, preferred_element_type=jnp.float32)
    below_part = column_dot(below_coef, image_half).astype(jnp.bfloat16)
    above_part = column_dot(above_coef, image_half).astype(jnp.bfloat16)
    handed_part = column_dot(handed_coef, image_half).astype(jnp.bfloat16)
    returned = with_halo(jnp.concatenate([below_part, above_part], axis=0), (("blk", 0),), num_rows)
    from_group = shifted(handed_part, "group", -1)
    text_sum = text_sum + returned[:num_rows].astype(jnp.float32)
    text_sum = text_sum + returned[3 * num_rows :].astype(jnp.float32)
    text_sum = text_sum + from_group.astype(jnp.float32)
    grad_image = (
        image_sum - image_unit * jnp.sum(image_unit * image_sum, axis=-1, keepdims=True)
    ) * image_inv
    grad_text = (
        text_sum - text_unit * jnp.sum(text_unit * text_sum, axis=-1, keepdims=True)
    ) * text_inv
    return (grad_image.astype(jnp.bfloat16), grad_text.astype(jnp.bfloat16))


def solution(mesh):
    placed = (
        P(("blk", "group"), None),
        P(("blk", "group"), None),
        P(("blk", "group"), None),
        P(),
        P(),
        P(),
    )
    return jax.shard_map(
        shards,
        mesh=mesh,
        in_specs=placed,
        out_specs=(P(("blk", "group"), None), P(("blk", "group"), None)),
        check_vma=False,
    )
```

profile of v0, /device:TPU:1, one launch (start us, length us, event | category | flops | bytes accessed | tf_op | source)
XLA Modules:
  0.0 167.0 jit_solution(16337770992410843503)
XLA Ops:
  0.6 0.0 copy-start
  0.6 0.0 copy-start.1
  0.7 3.4 %multiply_reduce_fusion.1 = f32[640]{0:T(1024)S(1)} fusion(s32[640,1152]{1,0:T(8,128)} %param.8, bf16[640,1152]{1,0:T(8,128)(2,1)} %param.7), kind=kLoop, calls=%fused_computation.19 | loop fusion | flops 7372160 | bytes 4426240 | tf_op jit(solution)/shard_map/reduce_sum | solution.py:33
  4.1 0.0 copy-done
  4.1 0.1 copy-done.1
  4.2 2.0 %multiply_convert_fusion.1 = bf16[640,1152]{1,0:T(8,128)(2,1)} fusion(f32[640]{0:T(1024)S(1)} %get-tuple-element.7, s32[640,1152]{1,0:T(8,128)S(1)} %copy-done, bf16[640,1152]{1,0:T(8,128)(2,1)S(1)} %copy-done.1), kind=kLoop, calls=%fused_computation.21 | loop fusion | flops 6635520 | bytes 5900800 | tf_op jit(solution)/shard_map/convert_element_type | solution.py:76
  6.2 2.1 %collective-permute-start.2 = (bf16[640,1152]{1,0:T(8,128)(2,1)}, bf16[640,1152]{1,0:T(8,128)(2,1)}, u32[]{:S(2)}, u32[]{:S(2)}) collective-permute-start(bf16[640,1152]{1,0:T(8,128)(2,1)} %multiply_convert_fusion.1), channel_id=1, source_target_pairs={{0,1},{1,2},{2,3},{3,4},{4,5},{5,6},{6,7},{7,0},{8,9},{9,10},{10,1... | collective-permute-start | bytes 4423688 | tf_op jit(solution)/shard_map/ppermute | solution.py:28
  8.3 3.5 %collective-permute-start = (bf16[640,1152]{1,0:T(8,128)(2,1)}, bf16[640,1152]{1,0:T(8,128)(2,1)}, u32[]{:S(2)}, u32[]{:S(2)}) collective-permute-start(bf16[640,1152]{1,0:T(8,128)(2,1)} %multiply_convert_fusion.1), channel_id=1, source_target_pairs={{0,8},{8,16},{16,24},{24,32},{32,40},{40,48},{48,56},{56,64},{64,7... | collective-permute-start | bytes 4423688 | tf_op jit(solution)/shard_map/ppermute | solution.py:16
  11.8 0.0 collective-permute-start.1
  13.1 0.9 fusion.18
  13.9 1.7 %fusion.8 = f32[640]{0:T(1024)S(1)} fusion(bf16[640,1152]{1,0:T(8,128)(2,1)} %param.6), kind=kLoop, calls=%fused_computation.15 | loop fusion | flops 2211200 | bytes 1477120 | tf_op jit(solution)/shard_map/reduce_sum | solution.py:33
  15.7 3.5 %multiply_convert_fusion.5 = bf16[640,640]{1,0:T(8,128)(2,1)S(1)} fusion(bf16[640,1152]{1,0:T(8,128)(2,1)} %multiply_convert_fusion.1, f32[]{:T(128)S(6)} %copy.9, f32[]{:T(128)S(6)} %copy.8, s32[640]{0:T(1024)S(1)} %get-tuple-element.4, bf16[640,1152]{1,0:T(8,128)(2,1)} %param.6, f32[640]{0:T(1024)S(1)} %add_rsqrt_fusion.1), kind=kOutput, calls=%fused_computation.25 | convolution fusion | flops 950845440 | bytes 3773448 | tf_op jit(solution)/shard_map/dot_general | solution.py:43
  19.2 0.0 copy-start.3
  19.2 2.9 %fusion.19 = f32[640,1152]{1,0:T(8,128)S(1)} fusion(bf16[640,640]{1,0:T(8,128)(2,1)S(1)} %multiply_convert_fusion.5, bf16[640,1152]{1,0:T(8,128)(2,1)} %multiply_convert_fusion.1), kind=kOutput, calls=%fused_computation.31 | convolution fusion | flops 943718400 | bytes 5242880 | tf_op jit(solution)/shard_map/dot_general | solution.py:86
  22.1 33.8 %collective-permute-done.2 = bf16[640,1152]{1,0:T(8,128)(2,1)} collective-permute-done((bf16[640,1152]{1,0:T(8,128)(2,1)}, bf16[640,1152]{1,0:T(8,128)(2,1)}, u32[]{:S(2)}, u32[]{:S(2)}) %collective-permute-start.2) | collective-permute-done | bytes 1474592 | tf_op jit(solution)/shard_map/ppermute | solution.py:28
  55.9 0.0 copy-done.3
  55.9 3.1 %multiply_convert_fusion.2 = bf16[640,640]{1,0:T(8,128)(2,1)S(1)} fusion(bf16[640,1152]{1,0:T(8,128)(2,1)} %collective-permute-done.2, s32[640]{0:T(1024)S(1)} %get-tuple-element.5, f32[]{:T(128)S(6)} %copy.9, f32[]{:T(128)S(6)} %copy.8, s32[640]{0:T(1024)S(1)} %get-tuple-element.4, bf16[640,1152]{1,0:T(8,128)(2,1)S(1)} %copy-done.3, ...), kind=kOutput, calls=%fused_computation.22 | convolution fusion | flops 950845440 | bytes 3776008 | tf_op jit(solution)/shard_map/dot_general | solution.py:43
  59.0 1.5 convolution_convert_fusion
  60.5 4.1 %collective-permute-start.5 = (bf16[640,1152]{1,0:T(8,128)(2,1)S(1)}, bf16[640,1152]{1,0:T(8,128)(2,1)S(1)}, u32[]{:S(2)}, u32[]{:S(2)}) collective-permute-start(bf16[640,1152]{1,0:T(8,128)(2,1)S(1)} %convolution_convert_fusion), channel_id=1, source_target_pairs={{0,7},{1,0},{2,1},{3,2},{4,3},{5,4},{6,5},{7,6},{8,15},{9,8},{10,9... | collective-permute-start | bytes 4423688 | tf_op jit(solution)/shard_map/ppermute | solution.py:28
  64.6 55.1 %collective-permute-done = bf16[640,1152]{1,0:T(8,128)(2,1)} collective-permute-done((bf16[640,1152]{1,0:T(8,128)(2,1)}, bf16[640,1152]{1,0:T(8,128)(2,1)}, u32[]{:S(2)}, u32[]{:S(2)}) %collective-permute-start) | collective-permute-done | bytes 1474592 | tf_op jit(solution)/shard_map/ppermute | solution.py:16
  119.7 3.1 %multiply_convert_fusion.4 = bf16[640,640]{1,0:T(8,128)(2,1)S(1)} fusion(bf16[640,1152]{1,0:T(8,128)(2,1)} %collective-permute-done, s32[640]{0:T(1024)S(1)} %get-tuple-element.3, f32[]{:T(128)S(6)} %copy.9, f32[]{:T(128)S(6)} %copy.8, s32[640]{0:T(1024)S(1)} %get-tuple-element.4, bf16[640,1152]{1,0:T(8,128)(2,1)S(1)} %copy-done.3, f32[640]{0:T(1024)S(1)} %add_rsqrt_fusion.1), kind=kOutput, calls=%fused_computation.24 | convolution fusion | flops 950845440 | bytes 3776008 | tf_op jit(solution)/shard_map/dot_general | solution.py:43
  122.8 1.5 convolution_convert_fusion.1
  124.3 0.1 collective-permute-start.4
  124.4 0.0 collective-permute-done.1
  124.4 3.1 %multiply_convert_fusion.3 = bf16[640,640]{1,0:T(8,128)(2,1)S(1)} fusion(bf16[640,1152]{1,0:T(8,128)(2,1)} %collective-permute-done.1, s32[640]{0:T(1024)S(1)} %get-tuple-element.2, f32[]{:T(128)S(6)} %copy.9, f32[]{:T(128)S(6)} %copy.8, s32[640]{0:T(1024)S(1)} %get-tuple-element.4, bf16[640,1152]{1,0:T(8,128)(2,1)S(1)} %copy-done.3, ...), kind=kOutput, calls=%fused_computation.23 | convolution fusion | flops 950845440 | bytes 3776008 | tf_op jit(solution)/shard_map/dot_general | solution.py:43
  127.5 1.5 convolution_convert_fusion.2
  129.0 4.3 %collective-permute-start.3 = (bf16[640,1152]{1,0:T(8,128)(2,1)S(1)}, bf16[640,1152]{1,0:T(8,128)(2,1)S(1)}, u32[]{:S(2)}, u32[]{:S(2)}) collective-permute-start(bf16[640,1152]{1,0:T(8,128)(2,1)S(1)} %convolution_convert_fusion.2), channel_id=1, source_target_pairs={{0,8},{8,16},{16,24},{24,32},{32,40},{40,48},{48,56},{56,64},{64,7... | collective-permute-start | bytes 4423688 | tf_op jit(solution)/shard_map/ppermute | solution.py:16
  133.3 2.9 %convolution_add_fusion.1 = f32[640,1152]{1,0:T(8,128)S(1)} fusion(f32[640,1152]{1,0:T(8,128)S(1)} %fusion.19, bf16[640,640]{1,0:T(8,128)(2,1)S(1)} %multiply_convert_fusion.4, bf16[640,1152]{1,0:T(8,128)(2,1)} %collective-permute-done), kind=kOutput, calls=%fused_computation.1 | convolution fusion | flops 944455680 | bytes 8192000 | tf_op jit(solution)/shard_map/dot_general | solution.py:91
  136.1 2.8 %fusion.20 = f32[640,1152]{1,0:T(8,128)S(1)} fusion(bf16[640,640]{1,0:T(8,128)(2,1)S(1)} %multiply_convert_fusion.2, bf16[640,1152]{1,0:T(8,128)(2,1)} %collective-permute-done.2), kind=kOutput, calls=%fused_computation.32 | convolution fusion | flops 943718400 | bytes 5242880 | tf_op jit(solution)/shard_map/dot_general | solution.py:93
  138.9 3.1 %fusion.4 = (f32[640]{0:T(1024)S(1)}, f32[640,1152]{1,0:T(8,128)S(1)}) fusion(bf16[640,1152]{1,0:T(8,128)(2,1)S(1)} %copy-done.3, f32[640]{0:T(1024)S(1)} %add_rsqrt_fusion.1, f32[640,1152]{1,0:T(8,128)S(1)} %fusion.20, f32[640,1152]{1,0:T(8,128)S(1)} %convolution_add_fusion.1, bf16[640,640]{1,0:T(8,128)(2,1)S(1)} %multiply_convert_fusion.3, ...), kind=kOutput, calls=%fused_computation.11 | convolution fusion | flops 948141440 | bytes 12620800 | tf_op jit(solution)/shard_map/dot_general | solution.py:92
  142.0 0.0 copy-start.2
  142.0 1.7 %fusion.7 = bf16[640,1152]{1,0:T(8,128)(2,1)} fusion(f32[640,1152]{1,0:T(8,128)S(1)} %get-tuple-element.9, bf16[640,1152]{1,0:T(8,128)(2,1)S(1)} %copy-done.3, f32[640]{0:T(1024)S(1)} %get-tuple-element.8, f32[640]{0:T(1024)S(1)} %add_rsqrt_fusion.1), kind=kLoop, calls=%fused_computation.14 | loop fusion | flops 4423680 | bytes 5903360 | tf_op jit(solution)/shard_map/convert_element_type | solution.py:108
  143.7 0.0 collective-permute-done.5
  143.7 17.5 %collective-permute-done.4 = bf16[640,1152]{1,0:T(8,128)(2,1)S(1)} collective-permute-done((bf16[640,1152]{1,0:T(8,128)(2,1)S(1)}, bf16[640,1152]{1,0:T(8,128)(2,1)S(1)}, u32[]{:S(2)}, u32[]{:S(2)}) %collective-permute-start.4) | collective-permute-done | bytes 1474592 | tf_op jit(solution)/shard_map/ppermute | solution.py:18
  161.2 0.0 collective-permute-done.3
  161.2 0.0 copy-done.2
  161.2 2.9 %multiply_reduce_fusion = (f32[640]{0:T(1024)S(1)}, f32[640,1152]{1,0:T(8,128)S(1)}) fusion(f32[640]{0:T(1024)S(1)} %get-tuple-element.7, bf16[640,1152]{1,0:T(8,128)(2,1)S(1)} %collective-permute-done.5, bf16[640,1152]{1,0:T(8,128)(2,1)S(1)} %collective-permute-done.4, bf16[640,1152]{1,0:T(8,128)(2,1)S(1)} %collective-permute-done.3, ...), kind=kOutput, calls=%fused_computation.17 | convolution fusion | flops 957726080 | bytes 14097920 | tf_op jit(solution)/shard_map/dot_general | solution.py:49
  164.1 2.9 %multiply_convert_fusion = bf16[640,1152]{1,0:T(8,128)(2,1)} fusion(f32[640]{0:T(1024)S(1)} %get-tuple-element.6, f32[640]{0:T(1024)S(1)} %get-tuple-element.10, f32[640]{0:T(1024)S(1)} %get-tuple-element.7, bf16[640,1152]{1,0:T(8,128)(2,1)S(1)} %collective-permute-done.5, bf16[640,1152]{1,0:T(8,128)(2,1)S(1)} %collective-permute-done.4, ...), kind=kLoop, calls=%fused_computation.16 | loop fusion | flops 13271040 | bytes 13278720 | tf_op jit(solution)/shard_map/convert_element_type | solution.py:108
  (2 shorter events, 0.0 us)
Async XLA Ops:
  0.6 3.5 %copy-start = (s32[640,1152]{1,0:T(8,128)S(1)}, s32[640,1152]{1,0:T(8,128)}, u32[]{:S(2)}) copy-start(s32[640,1152]{1,0:T(8,128)} %param.8) | copy-start | bytes 8847364
  0.6 3.6 %copy-start.1 = (bf16[640,1152]{1,0:T(8,128)(2,1)S(1)}, bf16[640,1152]{1,0:T(8,128)(2,1)}, u32[]{:S(2)}) copy-start(bf16[640,1152]{1,0:T(8,128)(2,1)} %param.7) | copy-start | bytes 4423684
  6.2 49.8 %collective-permute-start.2 = (bf16[640,1152]{1,0:T(8,128)(2,1)}, bf16[640,1152]{1,0:T(8,128)(2,1)}, u32[]{:S(2)}, u32[]{:S(2)}) collective-permute-start(bf16[640,1152]{1,0:T(8,128)(2,1)} %multiply_convert_fusion.1), channel_id=1, source_target_pairs={{0,1},{1,2},{2,3},{3,4},{4,5},{5,6},{6,7},{7,0},{8,9},{9,10},{10,1... | collective-permute-start | bytes 4423688 | tf_op jit(solution)/shard_map/ppermute | solution.py:28
  8.3 111.4 %collective-permute-start = (bf16[640,1152]{1,0:T(8,128)(2,1)}, bf16[640,1152]{1,0:T(8,128)(2,1)}, u32[]{:S(2)}, u32[]{:S(2)}) collective-permute-start(bf16[640,1152]{1,0:T(8,128)(2,1)} %multiply_convert_fusion.1), channel_id=1, source_target_pairs={{0,8},{8,16},{16,24},{24,32},{32,40},{40,48},{48,56},{56,64},{64,7... | collective-permute-start | bytes 4423688 | tf_op jit(solution)/shard_map/ppermute | solution.py:16
  11.8 112.6 %collective-permute-start.1 = (bf16[640,1152]{1,0:T(8,128)(2,1)}, bf16[640,1152]{1,0:T(8,128)(2,1)}, u32[]{:S(2)}, u32[]{:S(2)}) collective-permute-start(bf16[640,1152]{1,0:T(8,128)(2,1)} %multiply_convert_fusion.1), channel_id=1, source_target_pairs={{8,0},{16,8},{24,16},{32,24},{40,32},{48,40},{56,48},{64,56},{72,6... | collective-permute-start | bytes 4423688 | tf_op jit(solution)/shard_map/ppermute | solution.py:18
  19.2 36.8 %copy-start.3 = (bf16[640,1152]{1,0:T(8,128)(2,1)S(1)}, bf16[640,1152]{1,0:T(8,128)(2,1)}, u32[]{:S(2)}) copy-start(bf16[640,1152]{1,0:T(8,128)(2,1)} %param.6) | copy-start | bytes 4423684
  60.5 83.2 %collective-permute-start.5 = (bf16[640,1152]{1,0:T(8,128)(2,1)S(1)}, bf16[640,1152]{1,0:T(8,128)(2,1)S(1)}, u32[]{:S(2)}, u32[]{:S(2)}) collective-permute-start(bf16[640,1152]{1,0:T(8,128)(2,1)S(1)} %convolution_convert_fusion), channel_id=1, source_target_pairs={{0,7},{1,0},{2,1},{3,2},{4,3},{5,4},{6,5},{7,6},{8,15},{9,8},{10,9... | collective-permute-start | bytes 4423688 | tf_op jit(solution)/shard_map/ppermute | solution.py:28
  124.3 36.9 %collective-permute-start.4 = (bf16[640,1152]{1,0:T(8,128)(2,1)S(1)}, bf16[640,1152]{1,0:T(8,128)(2,1)S(1)}, u32[]{:S(2)}, u32[]{:S(2)}) collective-permute-start(bf16[640,1152]{1,0:T(8,128)(2,1)S(1)} %convolution_convert_fusion.1), channel_id=1, source_target_pairs={{8,0},{16,8},{24,16},{32,24},{40,32},{48,40},{56,48},{64,56},{72,6... | collective-permute-start | bytes 4423688 | tf_op jit(solution)/shard_map/ppermute | solution.py:18
  129.0 32.2 %collective-permute-start.3 = (bf16[640,1152]{1,0:T(8,128)(2,1)S(1)}, bf16[640,1152]{1,0:T(8,128)(2,1)S(1)}, u32[]{:S(2)}, u32[]{:S(2)}) collective-permute-start(bf16[640,1152]{1,0:T(8,128)(2,1)S(1)} %convolution_convert_fusion.2), channel_id=1, source_target_pairs={{0,8},{8,16},{16,24},{24,32},{32,40},{40,48},{48,56},{56,64},{64,7... | collective-permute-start | bytes 4423688 | tf_op jit(solution)/shard_map/ppermute | solution.py:16
  142.0 19.2 %copy-start.2 = (bf16[640,1152]{1,0:T(8,128)(2,1)S(1)}, bf16[640,1152]{1,0:T(8,128)(2,1)}, u32[]{:S(2)}) copy-start(bf16[640,1152]{1,0:T(8,128)(2,1)} %param.7) | copy-start | bytes 4423684
where the time goes:
time: 167 us
  waiting for transfers between devices  106 us (63%)
  matrix products  31.7 us (19%)
  starting transfers between devices  14.1 us (8%)
  other arithmetic  11.7 us (7%)
  between operations  2.08 us (1%)
    ppermute x2, waiting for transfers between devices, with_halo(): lax.ppermute(tail, axis, [(i, (i + 1) % count) for i in range(count)])  55.1 us
    ppermute x2, waiting for transfers between devices, shifted(): return lax.ppermute(value, axis, pairs)  33.8 us
    ppermute x2, waiting for transfers between devices, with_halo(): lax.ppermute(head, axis, [((i + 1) % count, i) for i in range(count)])  17.5 us
    dot_general x4, matrix products, pair_dot(): lax.dot_general(left, right, (((1,), (1,)), ((), ())), preferred_element_...  12.7 us
    ppermute x2, starting transfers between devices, with_halo(): lax.ppermute(tail, axis, [(i, (i + 1) % count) for i in range(count)])  7.76 us
    dot_general x4, matrix products, column_dot(): lax.dot_general(left, right, (((0,), (0,)), ((), ())), preferred_element_...  7.4 us
    ppermute x2, starting transfers between devices, shifted(): return lax.ppermute(value, axis, pairs)  6.23 us
    reduce_sum x2, other arithmetic, unit_rows(): inverse = lax.rsqrt(jnp.sum(full * full, axis=-1, keepdims=True) + EPS)  5.16 us
  transfers between devices with their start and end apart: 6, of which 3 were waited for; matrix products, arithmetic and copies ran while one was open for 20% of the time, Pallas kernels for 0%

commit v1 on v0

v1 whole, which is shorter than its diff:
```python
import functools

import jax
import jax.numpy as jnp
from jax import lax
from jax.experimental import pallas as pl
from jax.experimental.pallas import tpu as pltpu
from jax.sharding import PartitionSpec as P

EPS = 1e-06
LOG2E = 1.4426950408889634
MESH = pl.DeviceIdType.MESH

ROWS = 640
D = 1152
CHUNK = 128
SUB = 32
UNIT = ROWS // SUB
TILE = 320
PREP = 64
SET = 4 * ROWS
SPARE = 2 * SET
LAB = ROWS // 128


def kernel(
    n_blk,
    n_group,
    image_ref,
    text_ref,
    bits_ref,
    labels_ref,
    scale_ref,
    bias_ref,
    grad_image_ref,
    grad_text_ref,
    held,
    raw_image,
    raw_text,
    bits,
    labels,
    column,
    inverse,
    total,
    result,
    load_sem,
    label_sem,
    store_sem,
    near_send,
    near_recv,
    first_send,
    first_recv,
    far_send,
    far_recv,
    side_send,
    side_recv,
):
    b = lax.axis_index("blk")
    g = lax.axis_index("group")
    core = b % 2
    low = g % 2
    twin = b + 1 - 2 * core
    beyond = (b + 2 * core - 1 + n_blk) % n_blk
    mate = g + 1 - 2 * low
    side_to = (g + 2 - 4 * low + n_group) % n_group
    side_from = (g - 2 + 4 * low + n_group) % n_group
    near_dev, first_dev = (twin, g), (b, mate)
    far_dev, side_dev, source_dev = (beyond, mate), (b, side_to), (b, side_from)

    def load(array, to, piece, sems):
        rows = pl.ds(piece * PREP, PREP)
        return pltpu.make_async_copy(array.at[rows], to.at[rows], sems.at[piece])

    pieces = ROWS // PREP
    loads = ((image_ref, raw_image), (text_ref, raw_text), (bits_ref, bits))
    for which, (array, to) in enumerate(loads):
        for piece in range(pieces):
            load(array, to, piece, load_sem.at[which]).start()
    label_copy = pltpu.make_async_copy(labels_ref, labels, label_sem)
    label_copy.start()

    barrier = pltpu.get_barrier_semaphore()
    for device in (near_dev, first_dev, far_dev, source_dev):
        pl.semaphore_signal(barrier, inc=1, device_id=device, device_id_type=MESH)

    def remote(src, dst, send, recv, device):
        return pltpu.make_async_remote_copy(
            src_ref=held.at[src],
            dst_ref=held.at[dst],
            send_sem=send,
            recv_sem=recv,
            device_id=device,
            device_id_type=MESH,
        )

    def span(start, size):
        return pl.ds(pl.multiple_of(start, 16), size)

    def first_row(h, to_low):
        texts = h // UNIT
        at = h - texts * UNIT
        chunk = at // (CHUNK // SUB)
        inside = (at - chunk * (CHUNK // SUB)) * SUB
        used = texts * to_low + (1 - texts) * (1 - to_low)
        there = (1 - texts) * SET + 2 * ROWS + chunk * 2 * CHUNK + CHUNK
        return used * there + (1 - used) * (SPARE + chunk * CHUNK) + inside

    def first(h):
        texts = h // UNIT
        at = h - texts * UNIT
        return remote(
            span((1 - texts) * SET + at * SUB, SUB),
            span(first_row(h, 1 - low), SUB),
            first_send,
            first_recv.at[h],
            first_dev,
        )

    def landing(h):
        texts = h // UNIT
        at = h - texts * UNIT
        chunk = at // (CHUNK // SUB)
        inside = (at - chunk * (CHUNK // SUB)) * SUB
        return texts, chunk, (1 - texts) * SET + 2 * ROWS + chunk * 2 * CHUNK + inside

    def far(h):
        texts, chunk, row = landing(h)
        return remote(
            span(first_row(h, low), SUB),
            span(row, SUB),
            far_send,
            far_recv.at[texts * LAB + chunk],
            far_dev,
        )

    def side(h):
        texts, chunk, row = landing(h)
        return remote(
            span(first_row(h, low), SUB),
            span(row + CHUNK, SUB),
            side_send,
            side_recv.at[chunk],
            side_dev,
        )

    def near(texts):
        start = (1 - texts) * SET
        return remote(
            span(start, ROWS),
            span(start + ROWS, ROWS),
            near_send.at[texts],
            near_recv.at[texts],
            near_dev,
        )

    def unit_rows(full, row, which, base):
        inv = lax.rsqrt(jnp.sum(full * full, axis=-1, keepdims=True) + EPS)
        inverse[which, pl.ds(row, PREP), :] = inv
        held[pl.ds(base + row, PREP), :] = (full * inv).astype(jnp.bfloat16)

    def prepare_image(piece):
        load(image_ref, raw_image, piece, load_sem.at[0]).wait()
        row = pl.multiple_of(piece * PREP, PREP)
        unit_rows(raw_image[pl.ds(row, PREP), :].astype(jnp.float32), row, 0, SET)

    def prepare_text(piece):
        load(text_ref, raw_text, piece, load_sem.at[1]).wait()
        load(bits_ref, bits, piece, load_sem.at[2]).wait()
        row = pl.multiple_of(piece * PREP, PREP)
        rows = pl.ds(row, PREP)
        noise = (bits[rows, :].astype(jnp.float32) + 0.5) * (1.0 / 4096.0)
        full = jnp.floor(raw_text[rows, :].astype(jnp.float32) * 128.0 + noise) * (1.0 / 128.0)
        raw_text[rows, :] = full.astype(jnp.bfloat16)
        unit_rows(full, row, 1, 0)

    def clear(i, _):
        total[0, pl.ds(pl.multiple_of(i * PREP, PREP), PREP), :] = jnp.zeros((PREP, D), jnp.float32)
        total[1, pl.ds(pl.multiple_of(i * PREP, PREP), PREP), :] = jnp.zeros((PREP, D), jnp.float32)
        return 0

    prepare_image(0)
    pl.semaphore_wait(barrier, 4)

    per = PREP // SUB

    def image_step(piece, _):
        def send(i, _):
            first(piece * per + i).start()
            return 0

        lax.fori_loop(0, per, send, 0)

        @pl.when(piece + 1 < pieces)
        def _():
            prepare_image(piece + 1)

        return 0

    lax.fori_loop(0, pieces, image_step, 0)
    near(0).start()

    def text_step(piece, _):
        prepare_text(piece)

        def send(i, _):
            first(UNIT + piece * per + i).start()
            return 0

        lax.fori_loop(0, per, send, 0)
        return 0

    lax.fori_loop(0, pieces, text_step, 0)
    near(1).start()

    label_copy.wait()
    number = b * n_group + g
    for part in range(LAB):
        row = jnp.broadcast_to(labels[pl.ds(number * LAB + part, 1), :], (128, 128))
        column[pl.ds(part * 128, 128), :] = row.T

    lax.fori_loop(0, pieces, clear, 0)

    scale = scale_ref[0]
    slope = scale * LOG2E
    shift = bias_ref[0] * LOG2E
    below = (g - 1 + n_group) % n_group
    above = (g + 1) % n_group

    def pump(h):
        first(h).wait_recv()
        far(h).start()

        @pl.when(h // UNIT == 1 - low)
        def _():
            side(h).start()

    def meet(which, j, tile):
        far_chunk = j // LAB
        k = j - far_chunk * LAB
        own_part = 2 * k
        group = which * above + (1 - which) * below
        a_near = own_part // LAB
        b_near = (own_part + 1) // LAB
        num_a = (b + (twin - b) * a_near) * n_group + g
        num_b = (b + (twin - b) * b_near) * n_group + g
        row_a = num_a * LAB + own_part - a_near * LAB
        row_b = num_b * LAB + own_part + 1 - b_near * LAB
        far_a = (beyond * n_group + g) * LAB + k
        far_b = (b * n_group + group) * LAB + k
        row_a = row_a + (far_a - row_a) * far_chunk
        row_b = row_b + (far_b - row_b) * far_chunk
        them_rows = span(which * SET + j * 2 * CHUNK, 2 * CHUNK)
        own_rows = span((1 - which) * SET + tile * TILE, TILE)
        acc_rows = span(tile * TILE, TILE)
        dots = lax.dot_general(
            held[own_rows, :],
            held[them_rows, :],
            (((1,), (1,)), ((), ())),
            preferred_element_type=jnp.float32,
        )
        power = dots * slope + shift
        mine = column[acc_rows, :]
        same_a = mine == labels[pl.ds(row_a, 1), :]
        same_b = mine == labels[pl.ds(row_b, 1), :]
        same = jnp.concatenate([same_a, same_b], axis=1)
        coef = jnp.where(same, -scale, scale) / (1.0 + jnp.exp2(jnp.where(same, power, -power)))
        total[which, acc_rows, :] += lax.dot_general(
            coef.astype(jnp.bfloat16),
            held[them_rows, :],
            (((1,), (0,)), ((), ())),
            preferred_element_type=jnp.float32,
        )

    def finish(which, piece):
        row = pl.multiple_of(piece * PREP, PREP)
        rows = pl.ds(row, PREP)
        inv = inverse[which, rows, :]
        raw = raw_image if which == 0 else raw_text
        out = grad_image_ref if which == 0 else grad_text_ref
        unit = raw[rows, :].astype(jnp.float32) * inv
        sums = total[which, rows, :]
        along = jnp.sum(unit * sums, axis=-1, keepdims=True)
        result[which, rows, :] = ((sums - unit * along) * inv).astype(jnp.bfloat16)
        store(which, piece).start()

    def store(which, piece):
        out = grad_image_ref if which == 0 else grad_text_ref
        rows = pl.ds(piece * PREP, PREP)
        return pltpu.make_async_copy(result.at[which, rows], out.at[rows], store_sem.at[which, piece])

    def whole(start, size, send, recv):
        return remote(span(start, size), span(start, size), send, recv, first_dev)

    def landed(texts, k):
        base = (1 - texts) * SET + 2 * ROWS + k * 2 * CHUNK
        whole(base, CHUNK, far_send, far_recv.at[texts * LAB + k]).wait_recv()

        @pl.when(low == 1 - texts)
        def _():
            whole(base + CHUNK, CHUNK, side_send, side_recv.at[k]).wait_recv()

    tiles = ROWS // TILE

    def early(h, _):
        pump(h)
        p = h // tiles
        tile = h - p * tiles

        @pl.when(h == 4 * tiles)
        def _():
            near(0).wait_recv()
            near(1).wait_recv()

        meet(1 - p % 2, p // 2, tile)
        return 0

    lax.fori_loop(0, 2 * LAB * tiles, early, 0)
    done = 2 * LAB * tiles

    def middle(i, _):
        pump(done + i)
        k = i // tiles
        tile = i - k * tiles

        @pl.when(tile == 0)
        def _():
            landed(0, k)

        meet(1, LAB + k, tile)
        return 0

    lax.fori_loop(0, LAB * tiles, middle, 0)
    done = done + LAB * tiles

    def late(i, _):
        k = i // tiles
        tile = i - k * tiles

        @pl.when(i < 6)
        def _():
            pump(done + i)

        @pl.when((i >= 6) & (i < 8))
        def _():
            pump(done + 6 + 2 * (i - 6))
            pump(done + 7 + 2 * (i - 6))

        finish(1, i)

        @pl.when(tile == 0)
        def _():
            landed(1, k)

        meet(0, LAB + k, tile)
        return 0

    lax.fori_loop(0, LAB * tiles, late, 0)

    def last(piece, _):
        finish(0, piece)
        return 0

    lax.fori_loop(0, pieces, last, 0)

    near(0).wait_send()
    near(1).wait_send()
    whole(0, 2 * ROWS, first_send, first_recv.at[0]).wait_send()
    whole(0, 2 * ROWS, far_send, first_recv.at[0]).wait_send()
    whole(0, ROWS, side_send, first_recv.at[0]).wait_send()

    def stored(piece, _):
        store(0, piece).wait()
        store(1, piece).wait()
        return 0

    lax.fori_loop(0, pieces, stored, 0)


def shards(n_blk, n_group, image_embed, text_embed, text_bits, labels, scale, bias):
    dma = pltpu.SemaphoreType.DMA
    pieces = ROWS // PREP
    return pl.pallas_call(
        functools.partial(kernel, n_blk, n_group),
        out_shape=(
            jax.ShapeDtypeStruct((ROWS, D), jnp.bfloat16),
            jax.ShapeDtypeStruct((ROWS, D), jnp.bfloat16),
        ),
        in_specs=[pl.BlockSpec(memory_space=pl.ANY)] * 4
        + [pl.BlockSpec(memory_space=pltpu.SMEM)] * 2,
        out_specs=(pl.BlockSpec(memory_space=pl.ANY), pl.BlockSpec(memory_space=pl.ANY)),
        scratch_shapes=[
            pltpu.VMEM((SPARE + ROWS, D), jnp.bfloat16),
            pltpu.VMEM((ROWS, D), jnp.bfloat16),
            pltpu.VMEM((ROWS, D), jnp.bfloat16),
            pltpu.VMEM((ROWS, D), jnp.int32),
            pltpu.VMEM((labels.shape[0] // 128, 128), jnp.int32),
            pltpu.VMEM((ROWS, 128), jnp.int32),
            pltpu.VMEM((2, ROWS, 1), jnp.float32),
            pltpu.VMEM((2, ROWS, D), jnp.float32),
            pltpu.VMEM((2, ROWS, D), jnp.bfloat16),
            dma((3, pieces)),
            dma,
            dma((2, pieces)),
            dma((2,)),
            dma((2,)),
            dma,
            dma((2 * UNIT,)),
            dma,
            dma((2 * LAB,)),
            dma,
            dma((LAB,)),
        ],
        compiler_params=pltpu.CompilerParams(
            collective_id=0, has_side_effects=True, vmem_limit_bytes=48 * 1024 * 1024
        ),
    )(
        image_embed,
        text_embed,
        text_bits,
        labels.reshape(-1, 128),
        scale.reshape(1),
        bias.reshape(1),
    )


def solution(mesh):
    rows = P(("blk", "group"), None)
    return jax.shard_map(
        functools.partial(shards, mesh.shape["blk"], mesh.shape["group"]),
        mesh=mesh,
        in_specs=(rows, rows, rows, P(), P(), P()),
        out_specs=(rows, rows),
        check_vma=False,
    )
```

time: 167 us -> 95.2 us (0.57)
  waiting for transfers between devices: 106 us -> 0 us
  Pallas kernels: 0 us -> 88.4 us
  matrix products: 31.7 us -> 0 us
  starting transfers between devices: 14.1 us -> 0 us
  other arithmetic: 11.7 us -> 0 us
  local copies, waits for them, and re-layouts: 1 us -> 4.68 us
    ppermute x6 -> x0, waiting for transfers between devices: 106 us -> none  [the longest x2 55.1 us: with_halo(): lax.ppermute(tail, axis, [(i, (i + 1) % count) for i in range(count)])]
    pallas_call x0 -> x1, Pallas kernels: none -> 88.4 us  [shards(): pl.pallas_call(functools.partial(kernel, n_blk, n_group), out_shape=(jax....]
    dot_general x12 -> x0, matrix products: 31.7 us -> none  [the longest x4 12.7 us: pair_dot(): lax.dot_general(left, right, (((1,), (1,)), ((), ())), preferred_element_...]
    ppermute x6 -> x0, starting transfers between devices: 14.1 us -> none  [the longest x2 7.76 us: with_halo(): lax.ppermute(tail, axis, [(i, (i + 1) % count) for i in range(count)])]
    convert_element_type x3 -> x0, other arithmetic: 6.55 us -> none  [the longest x2 4.59 us: shards(): return (grad_image.astype(jnp.bfloat16), grad_text.astype(jnp.bfloat16))]
    reduce_sum x2 -> x0, other arithmetic: 5.16 us -> none  [unit_rows(): inverse = lax.rsqrt(jnp.sum(full * full, axis=-1, keepdims=True) + EPS)]
    unnamed x8 -> x6, local copies, waits for them, and re-layouts: 0.14 us -> 4.68 us
  transfers between devices with their start and end apart: 6 -> 0, of which waited for: 3 -> 0; matrix products, arithmetic and copies ran while one was open for 20% -> 0% of each run, Pallas kernels for 0% -> 0%
where the time goes in v1:
time: 95.2 us; the launch traced here: 95 us
  Pallas kernels  88.4 us (93%)
  local copies, waits for them, and re-layouts  4.68 us (5%)
  between operations  1.94 us (2%)
    pallas_call x1, Pallas kernels, shards(): pl.pallas_call(functools.partial(kernel, n_blk, n_group), out_shape=(jax....  88.4 us
    unnamed x6, local copies, waits for them, and re-layouts  4.68 us

profile of v1, /device:TPU:1, one launch (start us, length us, event | category | flops | bytes accessed | tf_op | source)
XLA Modules:
  0.0 95.0 jit_solution(3044311394190066520)
XLA Ops:
  1.9 0.0 copy-start
  1.9 1.4 %copy-done = bf16[640,1152]{1,0:T(8,128)(2,1)S(1)} copy-done((bf16[640,1152]{1,0:T(8,128)(2,1)S(1)}, bf16[640,1152]{1,0:T(8,128)(2,1)}, u32[]{:S(2)}) %copy-start) | copy-done | bytes 1474584
  3.3 0.0 copy-start.1
  3.3 1.1 %copy-done.1 = s32[163840]{0:T(1024)S(1)} copy-done((s32[163840]{0:T(1024)S(1)}, s32[163840]{0:T(1024)}, u32[]{:S(2)}) %copy-start.1) | copy-done | bytes 655384
  4.4 88.4 %shard_map.77 = (bf16[640,1152]{1,0:T(8,128)(2,1)S(1)}, bf16[640,1152]{1,0:T(8,128)(2,1)S(1)}) custom-call(bf16[640,1152]{1,0:T(8,128)(2,1)S(1)} %copy-done, bf16[640,1152]{1,0:T(8,128)(2,1)} %text_ref.1, s32[640,1152]{1,0:T(8,128)} %bits_ref.1, s32[1280,128]{1,0:T(8,128)S(1)} %bitcast.5, f32[1]{0:T(128)} %bitcast.3.scale_ref, f32[1]{0:T(128)} %bitcast.4.bias_ref), custom_call_target="tpu_custom_call" | custom-call | tf_op jit(solution)/shard_map/pallas_call | solution.py:382
  92.8 1.1 %copy.12 = bf16[640,1152]{1,0:T(8,128)(2,1)} copy(bf16[640,1152]{1,0:T(8,128)(2,1)S(1)} %get-tuple-element.4) | data formatting | bytes 2949120
  93.9 1.1 %copy.13 = bf16[640,1152]{1,0:T(8,128)(2,1)} copy(bf16[640,1152]{1,0:T(8,128)(2,1)S(1)} %get-tuple-element.5) | data formatting | bytes 2949120
Async XLA Ops:
  1.9 1.4 %copy-start = (bf16[640,1152]{1,0:T(8,128)(2,1)S(1)}, bf16[640,1152]{1,0:T(8,128)(2,1)}, u32[]{:S(2)}) copy-start(bf16[640,1152]{1,0:T(8,128)(2,1)} %image_ref.1) | copy-start | bytes 4423684
  3.3 1.1 %copy-start.1 = (s32[163840]{0:T(1024)S(1)}, s32[163840]{0:T(1024)}, u32[]{:S(2)}) copy-start(s32[163840]{0:T(1024)} %param.9) | copy-start | bytes 1966084

commit v2 on v1

v2 whole, which is shorter than its diff:
```python
import functools

import jax
import jax.numpy as jnp
from jax import lax
from jax.experimental import pallas as pl
from jax.experimental.pallas import tpu as pltpu
from jax.sharding import PartitionSpec as P

EPS = 1e-06
LOG2E = 1.4426950408889634
MESH = pl.DeviceIdType.MESH

ROWS = 640
D = 1152
HALF = 64
PAIR = 2 * HALF
SUB = 32
UNIT = ROWS // SUB
WIDE = 256
PREP = 128
STEP = 32
SET = 4 * ROWS
SPARE = 2 * SET
LAB = ROWS // 128
HALVES = ROWS // HALF
PAIRS = SET // PAIR
CHUNK = 2 * PAIR


def kernel(
    n_blk,
    n_group,
    image_ref,
    text_ref,
    bits_ref,
    labels_ref,
    scale_ref,
    bias_ref,
    grad_text,
    sums_image,
    raw_image,
    inverse_image,
    held,
    raw_text,
    bits,
    labels,
    column,
    table,
    inverse_text,
    sums_text,
    coefs,
    load_sem,
    label_sem,
    near_send,
    near_recv,
    first_send,
    first_recv,
    far_send,
    far_recv,
    side_send,
    side_recv,
):
    b = lax.axis_index("blk")
    g = lax.axis_index("group")
    core = b % 2
    low = g % 2
    twin = b + 1 - 2 * core
    beyond = (b + 2 * core - 1 + n_blk) % n_blk
    mate = g + 1 - 2 * low
    side_to = (g + 2 - 4 * low + n_group) % n_group
    side_from = (g - 2 + 4 * low + n_group) % n_group
    near_dev, first_dev = (twin, g), (b, mate)
    far_dev, side_dev, source_dev = (beyond, mate), (b, side_to), (b, side_from)

    barrier = pltpu.get_barrier_semaphore()
    for device in (near_dev, first_dev, far_dev, source_dev):
        pl.semaphore_signal(barrier, inc=1, device_id=device, device_id_type=MESH)

    def load(array, to, piece, sems):
        rows = pl.ds(piece * PREP, PREP)
        return pltpu.make_async_copy(array.at[rows], to.at[rows], sems.at[piece])

    pieces = ROWS // PREP
    loads = ((image_ref, raw_image), (text_ref, raw_text), (bits_ref, bits))
    for which, (array, to) in enumerate(loads):
        for piece in range(pieces):
            load(array, to, piece, load_sem.at[which]).start()
    label_copy = pltpu.make_async_copy(labels_ref, labels, label_sem)
    label_copy.start()

    def remote(src, dst, send, recv, device):
        return pltpu.make_async_remote_copy(
            src_ref=held.at[src],
            dst_ref=held.at[dst],
            send_sem=send,
            recv_sem=recv,
            device_id=device,
            device_id_type=MESH,
        )

    def span(start, size):
        return pl.ds(pl.multiple_of(start, 16), size)

    def landing(h):
        texts = h // UNIT
        at = h - texts * UNIT
        half = at // (HALF // SUB)
        inside = (at - half * (HALF // SUB)) * SUB
        return texts, half, (1 - texts) * SET + 2 * ROWS + half * PAIR + inside

    def first_row(h, to_low):
        texts, _, row = landing(h)
        at = h - texts * UNIT
        used = texts * to_low + (1 - texts) * (1 - to_low)
        return used * (row + HALF) + (1 - used) * (SPARE + at * SUB)

    def first(h):
        texts = h // UNIT
        at = h - texts * UNIT
        return remote(
            span((1 - texts) * SET + at * SUB, SUB),
            span(first_row(h, 1 - low), SUB),
            first_send,
            first_recv.at[h],
            first_dev,
        )

    def far(h):
        texts, half, row = landing(h)
        return remote(
            span(first_row(h, low), SUB),
            span(row, SUB),
            far_send,
            far_recv.at[texts * HALVES + half],
            far_dev,
        )

    def side(h):
        texts, half, row = landing(h)
        return remote(
            span(first_row(h, low), SUB),
            span(row + HALF, SUB),
            side_send,
            side_recv.at[half],
            side_dev,
        )

    def near(texts):
        start = (1 - texts) * SET
        return remote(
            span(start, ROWS),
            span(start + ROWS, ROWS),
            near_send.at[texts],
            near_recv.at[texts],
            near_dev,
        )

    def unit_rows(fulls, steps, inverse, base):
        invs = [
            lax.rsqrt(jnp.sum(jnp.square(full()), axis=-1, keepdims=True) + EPS) for full in fulls
        ]
        for full, inv, row in zip(fulls, invs, steps):
            inverse[pl.ds(row, STEP), :] = inv
            held[pl.ds(base + row, STEP), :] = (full() * inv).astype(jnp.bfloat16)

    def steps_of(row, size):
        return [pl.multiple_of(row + at, STEP) for at in range(0, size, STEP)]

    def loader(array, row):
        return lambda: array[pl.ds(row, STEP), :].astype(jnp.float32)

    def image_rows(row, size):
        steps = steps_of(row, size)
        unit_rows([loader(raw_image, at) for at in steps], steps, inverse_image, SET)

    def text_rows(row, size):
        steps = steps_of(row, size)
        for at in steps:
            rows = pl.ds(at, STEP)
            noise = (bits[rows, :].astype(jnp.float32) + 0.5) * (1.0 / 4096.0)
            full = jnp.floor(raw_text[rows, :].astype(jnp.float32) * 128.0 + noise) * (1.0 / 128.0)
            raw_text[rows, :] = full.astype(jnp.bfloat16)
        unit_rows([loader(raw_text, at) for at in steps], steps, inverse_text, 0)

    per = PREP // SUB

    def send(h, _):
        first(h).start()
        return 0

    load(image_ref, raw_image, 0, load_sem.at[0]).wait()
    image_rows(0, STEP)
    pl.semaphore_wait(barrier, 4)
    lax.fori_loop(0, STEP // SUB, send, 0)
    for row in range(STEP, PREP, STEP):
        image_rows(row, STEP)
        lax.fori_loop(row // SUB, (row + STEP) // SUB, send, 0)

    def image_step(piece, _):
        load(image_ref, raw_image, piece, load_sem.at[0]).wait()
        image_rows(piece * PREP, PREP)
        lax.fori_loop(piece * per, (piece + 1) * per, send, 0)
        return 0

    lax.fori_loop(1, pieces, image_step, 0)
    near(0).start()

    def pump(h):
        first(h).wait_recv()
        far(h).start()

        @pl.when(h // UNIT == 1 - low)
        def _():
            side(h).start()

    def pumps(start, stop):
        def one(h, _):
            pump(h)
            return 0

        lax.fori_loop(start, stop, one, 0)

    pumps(0, 1)

    def text_step(piece, _):
        load(text_ref, raw_text, piece, load_sem.at[1]).wait()
        load(bits_ref, bits, piece, load_sem.at[2]).wait()
        text_rows(piece * PREP, PREP)
        lax.fori_loop(UNIT + piece * per, UNIT + (piece + 1) * per, send, 0)

        @pl.when(piece % 2 == 0)
        def _():
            pump(1 + piece // 2)

        return 0

    lax.fori_loop(0, pieces, text_step, 0)
    near(1).start()

    label_copy.wait()
    number = b * n_group + g
    for part in range(LAB):
        row = jnp.broadcast_to(labels[pl.ds(number * LAB + part, 1), :], (128, 128))
        column[pl.ds(part * 128, 128), :] = row.T

    below = (g - 1 + n_group) % n_group
    above = (g + 1) % n_group
    first_half = lax.broadcasted_iota(jnp.int32, (1, PAIR), 1) < HALF

    def label_row(at_blk, at_group, part):
        return labels[pl.ds((at_blk * n_group + at_group) * LAB + part, 1), :]

    for which, other in ((0, below), (1, above)):
        for part in range(LAB):
            table[which, pl.ds(part, 1), :] = label_row(b, g, part)
            table[which, pl.ds(LAB + part, 1), :] = label_row(twin, g, part)
            far_labels = label_row(beyond, g, part)
            group_labels = label_row(b, other, part)
            table[which, pl.ds(2 * LAB + 2 * part, 1), :] = jnp.where(
                first_half, far_labels, pltpu.roll(group_labels, HALF, 1)
            )
            table[which, pl.ds(2 * LAB + 2 * part + 1, 1), :] = jnp.where(
                first_half, pltpu.roll(far_labels, HALF, 1), group_labels
            )

    scale = scale_ref[0]
    slope = scale * LOG2E
    shift = bias_ref[0] * LOG2E

    def meet(which, at, size):
        them_rows = span(which * SET + at * PAIR, size)
        own_rows = span((1 - which) * SET, ROWS)
        dots = lax.dot_general(
            held[own_rows, :],
            held[them_rows, :],
            (((1,), (1,)), ((), ())),
            preferred_element_type=jnp.float32,
        )
        power = dots * slope + shift
        mine = column[...]
        same = [mine == table[which, pl.ds(at + i, 1), :] for i in range(size // PAIR)]
        same = same[0] if size == PAIR else jnp.concatenate(same, axis=1)
        coef = jnp.where(same, -scale, scale) / (1.0 + jnp.exp2(jnp.where(same, power, -power)))
        columns = pl.ds(pl.multiple_of(at * PAIR, PAIR), size)
        coefs[which, :, columns] = coef.astype(jnp.bfloat16)

    def add_up(which, start, stop, column_at, width, fresh):
        rows = (stop - start) * PAIR
        columns = pl.ds(pl.multiple_of(column_at, 128), width)
        sums = lax.dot_general(
            coefs[which, :, pl.ds(start * PAIR, rows)],
            held[pl.ds(which * SET + start * PAIR, rows), columns],
            (((1,), (0,)), ((), ())),
            preferred_element_type=jnp.float32,
        )
        total = (sums_image, sums_text)[which]
        if not fresh:
            sums = sums + total[:, columns]
        total[:, columns] = sums

    full_columns = D // WIDE
    rest = D - full_columns * WIDE

    def whole(start, size, send, recv):
        return remote(span(start, size), span(start, size), send, recv, first_dev)

    def landed(texts, k):
        base = (1 - texts) * SET + 2 * ROWS + k * PAIR
        whole(base, HALF, far_send, far_recv.at[texts * HALVES + k]).wait_recv()

        @pl.when(low == 1 - texts)
        def _():
            whole(base + HALF, HALF, side_send, side_recv.at[k]).wait_recv()

    def meet_far(texts, k):
        landed(texts, 2 * k)
        landed(texts, 2 * k + 1)
        meet(1 - texts, 2 * LAB + 2 * k, CHUNK)

    def early(p, _):
        pump(4 + p)

        @pl.when(p == 4)
        def _():
            near(0).wait_recv()
            near(1).wait_recv()

        meet(1 - p % 2, 2 * (p // 2), CHUNK)
        return 0

    lax.fori_loop(0, 2 * LAB, early, 0)

    def far_images(k, _):
        pump(14 + k)
        meet_far(0, k)
        return 0

    lax.fori_loop(0, 3, far_images, 0)
    pumps(17, 19)

    def far_images_end(k, _):
        pumps(19 + 2 * (k - 3), 21 + 2 * (k - 3))
        meet_far(0, k)
        return 0

    lax.fori_loop(3, LAB, far_images_end, 0)

    def text_sums(n, _):
        pump(23 + n)
        add_up(1, 0, PAIRS, n * WIDE, WIDE, True)
        return 0

    lax.fori_loop(0, full_columns, text_sums, 0)
    pumps(27, 28)
    add_up(1, 0, PAIRS, full_columns * WIDE, rest, True)

    def text_out(piece, _):
        @pl.when(piece % 2 == 0)
        def _():
            pump(28 + piece // 2)

        finish_rows(raw_text, inverse_text, sums_text, grad_text, piece * PREP)
        return 0

    lax.fori_loop(0, pieces, text_out, 0)

    def far_texts(k, _):
        pump(31 + k)
        meet_far(1, k)
        return 0

    lax.fori_loop(0, 3, far_texts, 0)

    def image_sums(n, _):
        pump(34 + n)
        add_up(0, 0, PAIRS - 4, n * WIDE, WIDE, True)
        return 0

    lax.fori_loop(0, full_columns, image_sums, 0)
    pumps(38, 40)
    add_up(0, 0, PAIRS - 4, full_columns * WIDE, rest, True)

    meet_far(1, LAB - 2)
    landed(1, HALVES - 2)
    meet(0, PAIRS - 2, PAIR)
    add_up(0, PAIRS - 4, PAIRS - 1, 0, D, False)
    landed(1, HALVES - 1)
    meet(0, PAIRS - 1, PAIR)
    add_up(0, PAIRS - 1, PAIRS, 0, D, False)

    near(0).wait_send()
    near(1).wait_send()
    whole(0, 2 * ROWS, first_send, first_recv.at[0]).wait_send()
    whole(0, 2 * ROWS, far_send, first_recv.at[0]).wait_send()
    whole(0, ROWS, side_send, first_recv.at[0]).wait_send()


def finish_rows(raw, inverse, sums, out, row):
    steps = [pl.ds(pl.multiple_of(row + at, STEP), STEP) for at in range(0, PREP, STEP)]
    along = []
    for rows in steps:
        inv = inverse[rows, :]
        dot = jnp.sum(raw[rows, :].astype(jnp.float32) * sums[rows, :], axis=-1, keepdims=True)
        along.append((inv, inv * inv * dot))
    for rows, (inv, share) in zip(steps, along):
        full = raw[rows, :].astype(jnp.float32)
        out[rows, :] = ((sums[rows, :] - full * share) * inv).astype(jnp.bfloat16)


def finish_kernel(text, sums, raw, inverse, image_out, text_out, image, store_sem, text_sem):
    whole = pltpu.make_async_copy(text, text_out, text_sem)
    whole.start()

    def store(piece):
        rows = pl.ds(piece * PREP, PREP)
        return pltpu.make_async_copy(image.at[rows], image_out.at[rows], store_sem.at[piece])

    pieces = ROWS // PREP
    for piece in range(pieces):
        finish_rows(raw, inverse, sums, image, piece * PREP)
        store(piece).start()
    whole.wait()
    for piece in range(pieces):
        store(piece).wait()


def shards(n_blk, n_group, image_embed, text_embed, text_bits, labels, scale, bias):
    dma = pltpu.SemaphoreType.DMA
    pieces = ROWS // PREP
    fast = pl.BlockSpec(memory_space=pltpu.VMEM)
    parts = pl.pallas_call(
        functools.partial(kernel, n_blk, n_group),
        out_shape=(
            pltpu.VMEM((ROWS, D), jnp.bfloat16),
            pltpu.VMEM((ROWS, D), jnp.float32),
            pltpu.VMEM((ROWS, D), jnp.bfloat16),
            pltpu.VMEM((ROWS, 1), jnp.float32),
        ),
        in_specs=[pl.BlockSpec(memory_space=pl.ANY)] * 4
        + [pl.BlockSpec(memory_space=pltpu.SMEM)] * 2,
        out_specs=(fast,) * 4,
        scratch_shapes=[
            pltpu.VMEM((SPARE + ROWS, D), jnp.bfloat16),
            pltpu.VMEM((ROWS, D), jnp.bfloat16),
            pltpu.VMEM((ROWS, D), jnp.int32),
            pltpu.VMEM((labels.shape[0] // 128, 128), jnp.int32),
            pltpu.VMEM((ROWS, 128), jnp.int32),
            pltpu.VMEM((2, PAIRS, PAIR), jnp.int32),
            pltpu.VMEM((ROWS, 1), jnp.float32),
            pltpu.VMEM((ROWS, D), jnp.float32),
            pltpu.VMEM((2, ROWS, SET), jnp.bfloat16),
            dma((3, pieces)),
            dma,
            dma((2,)),
            dma((2,)),
            dma,
            dma((2 * UNIT,)),
            dma,
            dma((2 * HALVES,)),
            dma,
            dma((HALVES,)),
        ],
        compiler_params=pltpu.CompilerParams(
            collective_id=0, has_side_effects=True, vmem_limit_bytes=48 * 1024 * 1024
        ),
    )(
        *(
            pltpu.with_memory_space_constraint(array, pltpu.HBM)
            for array in (image_embed, text_embed, text_bits, labels.reshape(-1, 128))
        ),
        scale.reshape(1), bias.reshape(1),
    )
    block = jax.ShapeDtypeStruct((ROWS, D), jnp.bfloat16)
    return pl.pallas_call(
        finish_kernel,
        out_shape=(block, block),
        in_specs=[fast] * 4,
        out_specs=(pl.BlockSpec(memory_space=pl.ANY),) * 2,
        scratch_shapes=[pltpu.VMEM((ROWS, D), jnp.bfloat16), dma((pieces,)), dma],
        compiler_params=pltpu.CompilerParams(vmem_limit_bytes=16 * 1024 * 1024),
    )(*parts)


def solution(mesh):
    rows = P(("blk", "group"), None)
    return jax.shard_map(
        functools.partial(shards, mesh.shape["blk"], mesh.shape["group"]),
        mesh=mesh,
        in_specs=(rows, rows, rows, P(), P(), P()),
        out_specs=(rows, rows),
        check_vma=False,
    )
```

time: 95.2 us -> 82.6 us (0.87)
  Pallas kernels: 88.4 us -> 80.6 us
  local copies, waits for them, and re-layouts: 4.68 us -> 0 us
    pallas_call x1 -> x2, Pallas kernels: 88.4 us -> 80.6 us  [the longest x1 78.9 us: shards(): pl.pallas_call(functools.partial(kernel, n_blk, n_group), out_shape=(pltp...]
    unnamed x6 -> x0, local copies, waits for them, and re-layouts: 4.68 us -> none
where the time goes in v2:
time: 82.6 us; the launch traced here: 82.5 us
  Pallas kernels  80.6 us (98%)
  between operations  1.93 us (2%)
    pallas_call x1, Pallas kernels, shards(): pl.pallas_call(functools.partial(kernel, n_blk, n_group), out_shape=(pltp...  78.9 us

profile of v2, /device:TPU:1, one launch (start us, length us, event | category | flops | bytes accessed | tf_op | source)
XLA Modules:
  0.0 82.5 jit_solution(11598473502646344889)
XLA Ops:
  1.9 78.9 %shard_map.77 = (bf16[640,1152]{1,0:T(8,128)(2,1)S(1)}, f32[640,1152]{1,0:T(8,128)S(1)}, bf16[640,1152]{1,0:T(8,128)(2,1)S(1)}, f32[640,1]{1,0:T(8,128)S(1)}) custom-call(bf16[640,1152]{1,0:T(8,128)(2,1)} %image_ref.1, bf16[640,1152]{1,0:T(8,128)(2,1)} %text_ref.1, s32[640,1152]{1,0:T(8,128)} %bits_ref.1, s32[1280,128]{1,0:T(8,128)} %bitcast.5, ...), custom_call_target="tpu_custom_call" | custom-call | tf_op jit(solution)/shard_map/pallas_call | solution.py:432
  80.8 1.6 %shard_map.78 = (bf16[640,1152]{1,0:T(8,128)(2,1)}, bf16[640,1152]{1,0:T(8,128)(2,1)}) custom-call(bf16[640,1152]{1,0:T(8,128)(2,1)S(1)} %get-tuple-element.6.text, f32[640,1152]{1,0:T(8,128)S(1)} %get-tuple-element.7.sums, bf16[640,1152]{1,0:T(8,128)(2,1)S(1)} %get-tuple-element.8.raw, f32[640,1]{1,0:T(8,128)S(1)} %get-tuple-element.9.inverse), custom_call_target="tpu_custom_call" | custom-call | tf_op jit(solution)/shard_map/pallas_call | solution.py:475

commit v3 on v2

--- a/solution.py
+++ b/solution.py
@@ -19,6 +19,7 @@
 UNIT = ROWS // SUB
 WIDE = 256
 PREP = 128
+LAST = 128
 STEP = 32
 SET = 4 * ROWS
 SPARE = 2 * SET
@@ -41,6 +42,9 @@
     sums_image,
     raw_image,
     inverse_image,
+    along_image,
+    last_coef,
+    last_rows,
     held,
     raw_text,
     bits,
@@ -49,9 +53,11 @@
     table,
     inverse_text,
     sums_text,
+    along,
     coefs,
     load_sem,
     label_sem,
+    lead_sem,
     near_send,
     near_recv,
     first_send,
@@ -73,6 +79,17 @@
     near_dev, first_dev = (twin, g), (b, mate)
     far_dev, side_dev, source_dev = (beyond, mate), (b, side_to), (b, side_from)
 
+    def lead_copy(start, stop, sem):
+        rows = pl.ds(start, stop - start)
+        return pltpu.make_async_copy(image_ref.at[rows], raw_image.at[rows], sem)
+
+    leads = (
+        lead_copy(0, STEP, lead_sem.at[0]),
+        lead_copy(STEP, PREP, lead_sem.at[1]),
+    )
+    leads[0].start()
+    leads[1].start()
+
     barrier = pltpu.get_barrier_semaphore()
     for device in (near_dev, first_dev, far_dev, source_dev):
         pl.semaphore_signal(barrier, inc=1, device_id=device, device_id_type=MESH)
@@ -83,12 +100,14 @@
 
     pieces = ROWS // PREP
     loads = ((image_ref, raw_image), (text_ref, raw_text), (bits_ref, bits))
-    for which, (array, to) in enumerate(loads):
-        for piece in range(pieces):
-            load(array, to, piece, load_sem.at[which]).start()
+
+    def start_loads():
+        for which, (array, to) in enumerate(loads):
+            for piece in range(1 if which == 0 else 0, pieces):
+                load(array, to, piece, load_sem.at[which]).start()
+        label_copy.start()
+
     label_copy = pltpu.make_async_copy(labels_ref, labels, label_sem)
-    label_copy.start()
-
     def remote(src, dst, send, recv, device):
         return pltpu.make_async_remote_copy(
             src_ref=held.at[src],
@@ -189,10 +208,12 @@
         first(h).start()
         return 0
 
-    load(image_ref, raw_image, 0, load_sem.at[0]).wait()
+    leads[0].wait()
     image_rows(0, STEP)
     pl.semaphore_wait(barrier, 4)
     lax.fori_loop(0, STEP // SUB, send, 0)
+    start_loads()
+    leads[1].wait()
     for row in range(STEP, PREP, STEP):
         image_rows(row, STEP)
         lax.fori_loop(row // SUB, (row + STEP) // SUB, send, 0)
@@ -208,11 +229,12 @@
 
     def pump(h):
         first(h).wait_recv()
-        far(h).start()
 
         @pl.when(h // UNIT == 1 - low)
         def _():
             side(h).start()
+
+        far(h).start()
 
     def pumps(start, stop):
         def one(h, _):
@@ -268,7 +290,7 @@
     slope = scale * LOG2E
     shift = bias_ref[0] * LOG2E
 
-    def meet(which, at, size):
+    def meet(which, at, size, last=False):
         them_rows = span(which * SET + at * PAIR, size)
         own_rows = span((1 - which) * SET, ROWS)
         dots = lax.dot_general(
@@ -282,8 +304,16 @@
         same = [mine == table[which, pl.ds(at + i, 1), :] for i in range(size // PAIR)]
         same = same[0] if size == PAIR else jnp.concatenate(same, axis=1)
         coef = jnp.where(same, -scale, scale) / (1.0 + jnp.exp2(jnp.where(same, power, -power)))
-        columns = pl.ds(pl.multiple_of(at * PAIR, PAIR), size)
-        coefs[which, :, columns] = coef.astype(jnp.bfloat16)
+        coef = coef.astype(jnp.bfloat16)
+        share = coef.astype(jnp.float32) * dots
+        share = share[:, :PAIR] + share[:, PAIR:] if size == CHUNK else share
+        if last:
+            last_coef[...] = coef
+            along_image[...] = along[which] + share
+        else:
+            columns = pl.ds(pl.multiple_of(at * PAIR, PAIR), size)
+            coefs[which, :, columns] = coef
+            along[which] += share
 
     def add_up(which, start, stop, column_at, width, fresh):
         rows = (stop - start) * PAIR
@@ -318,6 +348,8 @@
         landed(texts, 2 * k + 1)
         meet(1 - texts, 2 * LAB + 2 * k, CHUNK)
 
+    along[...] = jnp.zeros_like(along)
+
     def early(p, _):
         pump(4 + p)
 
@@ -360,7 +392,8 @@
         def _():
             pump(28 + piece // 2)
 
-        finish_rows(raw_text, inverse_text, sums_text, grad_text, piece * PREP)
+        for at in range(0, PREP, STEP):
+            finish_rows(raw_text, inverse_text, along.at[1], sums_text, grad_text, piece * PREP + at, STEP)
         return 0
 
     lax.fori_loop(0, pieces, text_out, 0)
@@ -386,8 +419,8 @@
     meet(0, PAIRS - 2, PAIR)
     add_up(0, PAIRS - 4, PAIRS - 1, 0, D, False)
     landed(1, HALVES - 1)
-    meet(0, PAIRS - 1, PAIR)
-    add_up(0, PAIRS - 1, PAIRS, 0, D, False)
+    last_rows[...] = held[SET - PAIR : SET, :]
+    meet(0, PAIRS - 1, PAIR, last=True)
 
     near(0).wait_send()
     near(1).wait_send()
@@ -396,29 +429,33 @@
     whole(0, ROWS, side_send, first_recv.at[0]).wait_send()
 
 
-def finish_rows(raw, inverse, sums, out, row):
-    steps = [pl.ds(pl.multiple_of(row + at, STEP), STEP) for at in range(0, PREP, STEP)]
-    along = []
-    for rows in steps:
-        inv = inverse[rows, :]
-        dot = jnp.sum(raw[rows, :].astype(jnp.float32) * sums[rows, :], axis=-1, keepdims=True)
-        along.append((inv, inv * inv * dot))
-    for rows, (inv, share) in zip(steps, along):
-        full = raw[rows, :].astype(jnp.float32)
-        out[rows, :] = ((sums[rows, :] - full * share) * inv).astype(jnp.bfloat16)
-
-
-def finish_kernel(text, sums, raw, inverse, image_out, text_out, image, store_sem, text_sem):
+def finish_rows(raw, inverse, along, sums, out, row, size, more=None):
+    rows = pl.ds(pl.multiple_of(row, STEP), size)
+    inv = inverse[rows, :]
+    share = inv * jnp.sum(along[rows, :], axis=-1, keepdims=True)
+    total = sums[rows, :]
+    if more is not None:
+        total = total + more(rows)
+    full = raw[rows, :].astype(jnp.float32)
+    out[rows, :] = ((total - full * share) * inv).astype(jnp.bfloat16)
+
+
+def finish_kernel(
+    text, sums, raw, inverse, along, coef, others, image_out, text_out, image, store_sem, text_sem
+):
     whole = pltpu.make_async_copy(text, text_out, text_sem)
     whole.start()
 
     def store(piece):
-        rows = pl.ds(piece * PREP, PREP)
+        rows = pl.ds(piece * LAST, LAST)
         return pltpu.make_async_copy(image.at[rows], image_out.at[rows], store_sem.at[piece])
 
-    pieces = ROWS // PREP
+    def more(rows):
+        return jnp.dot(coef[rows, :], others[...], preferred_element_type=jnp.float32)
+
+    pieces = ROWS // LAST
     for piece in range(pieces):
-        finish_rows(raw, inverse, sums, image, piece * PREP)
+        finish_rows(raw, inverse, along, sums, image, piece * LAST, LAST, more)
         store(piece).start()
     whole.wait()
     for piece in range(pieces):
@@ -436,10 +473,13 @@
             pltpu.VMEM((ROWS, D), jnp.float32),
             pltpu.VMEM((ROWS, D), jnp.bfloat16),
             pltpu.VMEM((ROWS, 1), jnp.float32),
+            pltpu.VMEM((ROWS, PAIR), jnp.float32),
+            pltpu.VMEM((ROWS, PAIR), jnp.bfloat16),
+            pltpu.VMEM((PAIR, D), jnp.bfloat16),
         ),
         in_specs=[pl.BlockSpec(memory_space=pl.ANY)] * 4
         + [pl.BlockSpec(memory_space=pltpu.SMEM)] * 2,
-        out_specs=(fast,) * 4,
+        out_specs=(fast,) * 7,
         scratch_shapes=[
             pltpu.VMEM((SPARE + ROWS, D), jnp.bfloat16),
             pltpu.VMEM((ROWS, D), jnp.bfloat16),
@@ -449,9 +489,11 @@
             pltpu.VMEM((2, PAIRS, PAIR), jnp.int32),
             pltpu.VMEM((ROWS, 1), jnp.float32),
             pltpu.VMEM((ROWS, D), jnp.float32),
+            pltpu.VMEM((2, ROWS, PAIR), jnp.float32),
             pltpu.VMEM((2, ROWS, SET), jnp.bfloat16),
             dma((3, pieces)),
             dma,
+            dma((2,)),
             dma((2,)),
             dma((2,)),
             dma,
@@ -475,9 +517,9 @@
     return pl.pallas_call(
         finish_kernel,
         out_shape=(block, block),
-        in_specs=[fast] * 4,
+        in_specs=[fast] * 7,
         out_specs=(pl.BlockSpec(memory_space=pl.ANY),) * 2,
-        scratch_shapes=[pltpu.VMEM((ROWS, D), jnp.bfloat16), dma((pieces,)), dma],
+        scratch_shapes=[pltpu.VMEM((ROWS, D), jnp.bfloat16), dma((ROWS // LAST,)), dma],
         compiler_params=pltpu.CompilerParams(vmem_limit_bytes=16 * 1024 * 1024),
     )(*parts)
 

time: 82.6 us -> 82.6 us (level)
  no operation moved by 1% of the time
where the time goes in v3:
time: 82.6 us; the launch traced here: 82.4 us
  Pallas kernels  80.5 us (97%)
  between operations  1.93 us (2%)
    pallas_call x1, Pallas kernels, shards(): pl.pallas_call(functools.partial(kernel, n_blk, n_group), out_shape=(pltp...  78.8 us
    pallas_call x1, Pallas kernels, shards(): pl.pallas_call(finish_kernel, out_shape=(block, block), in_specs=[fast] *...  1.67 us

profile of v3, /device:TPU:1, one launch (start us, length us, event | category | flops | bytes accessed | tf_op | source)
XLA Modules:
  0.0 82.4 jit_solution(5425680698923564270)
XLA Ops:
  1.9 78.8 %shard_map.77 = (bf16[640,1152]{1,0:T(8,128)(2,1)S(1)}, f32[640,1152]{1,0:T(8,128)S(1)}, bf16[640,1152]{1,0:T(8,128)(2,1)S(1)}, f32[640,1]{1,0:T(8,128)S(1)}, f3...) custom-call(bf16[640,1152]{1,0:T(8,128)(2,1)} %image_ref.1, ...), custom_call_target="tpu_custom_call" | custom-call | tf_op jit(solution)/shard_map/pallas_call | solution.py:469
  80.8 1.7 %shard_map.78 = (bf16[640,1152]{1,0:T(8,128)(2,1)}, bf16[640,1152]{1,0:T(8,128)(2,1)}) custom-call(bf16[640,1152]{1,0:T(8,128)(2,1)S(1)} %get-tuple-element.9.text, f32[640,1152]{1,0:T(8,128)S(1)} %get-tuple-element.10.sums, bf16[640,1152]{1,0:T(8,128)(2,1)S(1)} %get-tuple-element.11.raw, f32[640,1]{1,0:T(8,128)S(1)} %get-tuple-element.12.inverse, ...), custom_call_target="tpu_custom_call" | custom-call | tf_op jit(solution)/shard_map/pallas_call | solution.py:517

commit v4 on v2

--- a/solution.py
+++ b/solution.py
@@ -17,6 +17,7 @@
 PAIR = 2 * HALF
 SUB = 32
 UNIT = ROWS // SUB
+LEAD = 2
 WIDE = 256
 PREP = 128
 STEP = 32
@@ -54,6 +55,7 @@
     label_sem,
     near_send,
     near_recv,
+    go_sem,
     first_send,
     first_recv,
     far_send,
@@ -121,7 +123,7 @@
         return remote(
             span((1 - texts) * SET + at * SUB, SUB),
             span(first_row(h, 1 - low), SUB),
-            first_send,
+            first_send.at[(h + 2 * UNIT - LEAD) // (2 * UNIT)],
             first_recv.at[h],
             first_dev,
         )
@@ -146,6 +148,9 @@
             side_dev,
         )
 
+    def whole(start, size, send, recv):
+        return remote(span(start, size), span(start, size), send, recv, first_dev)
+
     def near(texts):
         start = (1 - texts) * SET
         return remote(
@@ -192,11 +197,24 @@
     load(image_ref, raw_image, 0, load_sem.at[0]).wait()
     image_rows(0, STEP)
     pl.semaphore_wait(barrier, 4)
+
+    leads = b == 2
+    follows = b == 3
+
+    @pl.when(follows)
+    def _():
+        pl.semaphore_wait(go_sem, 1)
+
     lax.fori_loop(0, STEP // SUB, send, 0)
     for row in range(STEP, PREP, STEP):
         image_rows(row, STEP)
         lax.fori_loop(row // SUB, (row + STEP) // SUB, send, 0)
 
+    @pl.when(leads)
+    def _():
+        whole(0, LEAD * SUB, first_send.at[0], first_recv.at[0]).wait_send()
+        pl.semaphore_signal(go_sem, inc=1, device_id=near_dev, device_id_type=MESH)
+
     def image_step(piece, _):
         load(image_ref, raw_image, piece, load_sem.at[0]).wait()
         image_rows(piece * PREP, PREP)
@@ -204,6 +222,11 @@
         return 0
 
     lax.fori_loop(1, pieces, image_step, 0)
+
+    @pl.when(jnp.logical_not(leads))
+    def _():
+        whole(0, LEAD * SUB, first_send.at[0], first_recv.at[0]).wait_send()
+
     near(0).start()
 
     def pump(h):
@@ -302,9 +325,6 @@
     full_columns = D // WIDE
     rest = D - full_columns * WIDE
 
-    def whole(start, size, send, recv):
-        return remote(span(start, size), span(start, size), send, recv, first_dev)
-
     def landed(texts, k):
         base = (1 - texts) * SET + 2 * ROWS + k * PAIR
         whole(base, HALF, far_send, far_recv.at[texts * HALVES + k]).wait_recv()
@@ -391,7 +411,7 @@
 
     near(0).wait_send()
     near(1).wait_send()
-    whole(0, 2 * ROWS, first_send, first_recv.at[0]).wait_send()
+    whole(0, 2 * ROWS - LEAD * SUB, first_send.at[1], first_recv.at[0]).wait_send()
     whole(0, 2 * ROWS, far_send, first_recv.at[0]).wait_send()
     whole(0, ROWS, side_send, first_recv.at[0]).wait_send()
 
@@ -454,7 +474,8 @@
             dma,
             dma((2,)),
             dma((2,)),
-            dma,
+            pltpu.SemaphoreType.REGULAR,
+            dma((2,)),
             dma((2 * UNIT,)),
             dma,
             dma((2 * HALVES,)),

time: 82.6 us -> 81.1 us (0.982)
  Pallas kernels: 80.6 us -> 78.8 us
    pallas_call x1, Pallas kernels: 78.9 us -> 77.1 us  [shards(): pl.pallas_call(functools.partial(kernel, n_blk, n_group), out_shape=(pltp...]
where the time goes in v4:
time: 81.1 us; the launch traced here: 80.7 us
  Pallas kernels  78.8 us (97%)
  between operations  1.93 us (2%)
    pallas_call x1, Pallas kernels, shards(): pl.pallas_call(functools.partial(kernel, n_blk, n_group), out_shape=(pltp...  77.1 us
    pallas_call x1, Pallas kernels, shards(): pl.pallas_call(finish_kernel, out_shape=(block, block), in_specs=[fast] *...  1.64 us

profile of v4, /device:TPU:1, one launch (start us, length us, event | category | flops | bytes accessed | tf_op | source)
XLA Modules:
  0.0 80.7 jit_solution(2280483856029470463)
XLA Ops:
  1.9 77.1 %shard_map.77 = (bf16[640,1152]{1,0:T(8,128)(2,1)S(1)}, f32[640,1152]{1,0:T(8,128)S(1)}, bf16[640,1152]{1,0:T(8,128)(2,1)S(1)}, f32[640,1]{1,0:T(8,128)S(1)}) custom-call(bf16[640,1152]{1,0:T(8,128)(2,1)} %image_ref.1, bf16[640,1152]{1,0:T(8,128)(2,1)} %text_ref.1, s32[640,1152]{1,0:T(8,128)} %bits_ref.1, s32[1280,128]{1,0:T(8,128)} %bitcast.5, ...), custom_call_target="tpu_custom_call" | custom-call | tf_op jit(solution)/shard_map/pallas_call | solution.py:452
  79.1 1.6 %shard_map.78 = (bf16[640,1152]{1,0:T(8,128)(2,1)}, bf16[640,1152]{1,0:T(8,128)(2,1)}) custom-call(bf16[640,1152]{1,0:T(8,128)(2,1)S(1)} %get-tuple-element.6.text, f32[640,1152]{1,0:T(8,128)S(1)} %get-tuple-element.7.sums, bf16[640,1152]{1,0:T(8,128)(2,1)S(1)} %get-tuple-element.8.raw, f32[640,1]{1,0:T(8,128)S(1)} %get-tuple-element.9.inverse), custom_call_target="tpu_custom_call" | custom-call | tf_op jit(solution)/shard_map/pallas_call | solution.py:496
